TPU v7x, 256 devices: a whole 4x4x8 slice. The times are simulated.
256 devices in a mesh: dom: 256 (over z, y, x, core).
Axes of the slice: x: 4, y: 4, z: 8, core: 2. Of those that a mesh axis runs over, the one named last changes fastest.
Arguments:
- features: bfloat16 [64, 2097152], P(None, 'dom'), may hold values from -6 to 6
- cheb_weight: bfloat16 [4, 64, 64], replicated, may hold values from -0.375 to 0.375
- lap_tiles: bfloat16 [16384, 3, 128, 128], P('dom'), may hold values from -0.25 to 0.25
- col_index: int32 [16384, 3], P('dom'), may hold values from 0 to 63
- cross_tiles: bfloat16 [256, 5, 2, 128, 128], P('dom'), may hold values from -0.25 to 0.25
- send_index: int32 [256, 5, 2], P('dom'), may hold values from 0 to 63
- row_index: int32 [256, 5, 2], P('dom'), may hold values from 0 to 63
- pair_on: int32 [256, 5], P('dom'), may hold values 0 or 1
- blk_live: int32 [256], P('dom'), may hold values from 1 to 64, 12288 in all
- cotangent: bfloat16 [64, 2097152], P(None, 'dom'), may hold values from -6 to 6
Outputs:
- conv_out: bfloat16 [64, 2097152], P(None, 'dom')
- grad_x: bfloat16 [64, 2097152], P(None, 'dom')
- grad_w: float32 [4, 64, 64], replicated
Inputs may be any that keep to these rules, and one draw needn't show every extreme that they name: `blk_live`: the counts sum to 12288 and the largest is exactly 64.
All inputs are finite; a program needn't handle non-finite values. No bound on the sum of `pair_on` or of `blk_live` on one device may be relied on, other than what follows from the above.
Results may differ from a plain program's by a relative error of at most 0.0059.
Values may be sent and summed in bfloat16 or wider, within the bound.
A program may use at most 128 MiB of HBM per device.

v0:
```python
import functools

import jax
import jax.numpy as jnp
from jax import lax
from jax.experimental import pallas as pl
from jax.experimental.pallas import tpu as pltpu
from jax.sharding import PartitionSpec as P

F32 = jnp.float32
BF16 = jnp.bfloat16
I32 = jnp.int32
MESH = pl.DeviceIdType.MESH
GROUP = 16
CHUNKS = 8


def dot(a, b):
    return jnp.dot(a, b, preferred_element_type=F32)


def small_mod(value, count, largest):
    power = 1
    while power * 2 <= largest:
        power *= 2
    while power >= 1:
        step = count * power
        value = jnp.where(value >= step, value - step, value)
        power //= 2
    return value


def kernel(
    size,
    feat_hbm, cheb_ref, lap_hbm, col_vmem, col, cross_hbm, send_ref, row_ref, pair_ref, live_ref, cot_hbm,
    conv_hbm, gradx_hbm, gradw_ref,
    feat, cot, lap, lap_t, cross, cross_t, field, back, up, up_t, chain0, chain1, chain2, coup,
    send_f, recv_f, send_b, recv_b, conv, gradx, idx_v, idx, sends, rows, part, got1, mine2, got2, mine3, got3,
    load_sem, lap_sem, idx_sem, out_sem, sf_sem, rf_sem, sb_sem, rb_sem,
    s1_sem, r1_sem, s2_sem, r2_sem, s3_sem, r3_sem,
):
    blocks, width, block = lap.shape[0], feat.shape[0], lap.shape[2]
    nz = lap.shape[1]
    rounds = 5
    coups = 2 * rounds
    chains = (chain0, chain1, chain2)
    me = lax.axis_index("dom")
    near, far = me % GROUP, me // GROUP
    far_size = size // GROUP

    def partner(level):
        bit = (me // (1 << level)) % 2
        return me + (1 << level) * (1 - 2 * bit)

    def near_peer(step):
        return far * GROUP + (near + step) % GROUP

    def far_peer(step):
        return ((far + step) % far_size) * GROUP + near

    per = blocks // CHUNKS
    loads = [
        pltpu.make_async_copy(feat_hbm, feat, load_sem.at[0]),
        pltpu.make_async_copy(cot_hbm, cot, load_sem.at[1]),
        pltpu.make_async_copy(cross_hbm, cross, load_sem.at[2]),
    ]
    for load in loads:
        load.start()

    def lap_load(part_at):
        where = pl.ds(part_at * per, per)
        return pltpu.make_async_copy(lap_hbm.at[where], lap.at[where], lap_sem.at[part_at])

    for part_at in range(CHUNKS):
        lap_load(part_at).start()

    barrier = pltpu.get_barrier_semaphore()
    for level in range(rounds):
        pl.semaphore_signal(barrier, inc=1, device_id=(partner(level),), device_id_type=MESH)

    @pl.loop(1, GROUP)
    def _(step):
        pl.semaphore_signal(barrier, inc=1, device_id=(near_peer(step),), device_id_type=MESH)

    if far_size > 1:
        @pl.loop(1, far_size)
        def _(step):
            pl.semaphore_signal(barrier, inc=1, device_id=(far_peer(step),), device_id_type=MESH)

    live = live_ref[0]

    def mask_of(i):
        return (i < live).astype(F32)

    for k in range(coups):
        sends[0, k] = small_mod(send_ref[0, k // 2, k % 2], live, blocks - 1)
        rows[0, k] = small_mod(row_ref[0, k // 2, k % 2], live, blocks - 1)
    for table in (sends, rows):
        for k in range(coups):
            before = jnp.int32(coups)
            for other in range(k):
                before = jnp.where(table[0, other] == table[0, k], other, before)
            table[1, k] = before
    at_sub = lax.broadcasted_iota(I32, (blocks, 128), 0)
    at_lane = lax.broadcasted_iota(I32, (blocks, 128), 1)
    lane = lax.broadcasted_iota(I32, (1, 128), 1)
    for n in range(nz):
        cols = jnp.broadcast_to(col_vmem[:, n : n + 1], (blocks, 128))
        turned = jnp.sum(jnp.where(at_sub == at_lane, cols, 0), axis=0, keepdims=True)
        same = (cols == turned) & (at_sub < at_lane)
        prev = jnp.max(jnp.where(same, at_sub, -1), axis=0, keepdims=True)
        last = jnp.max(jnp.where(cols == at_lane, at_sub, -1), axis=0, keepdims=True)
        idx_v[n : n + 1, :] = jnp.where(prev < 0, blocks, prev)
        idx_v[nz + n : nz + n + 1, :] = jnp.where(last < 0, blocks, last)
    for at, table in ((6, rows), (7, sends)):
        last = jnp.full((1, 128), coups, I32)
        for k in range(coups):
            last = jnp.where(lane == table[0, k], k, last)
        idx_v[at : at + 1, :] = last
    idx_copy = pltpu.make_async_copy(idx_v, idx, idx_sem)
    idx_copy.start()

    zero_block = jnp.zeros((width, block), F32)
    for chain in chains:
        chain[blocks] = zero_block
    coup[coups] = zero_block
    cheb = cheb_ref[...]
    cheb_all = jnp.concatenate([cheb[k].T for k in range(4)], axis=1)

    def lanes(i):
        return pl.ds(pl.multiple_of(i * block, block), block)

    def forward_copy(at, level):
        pair = pl.ds(2 * level, 2)
        return pltpu.make_async_remote_copy(
            src_ref=send_f.at[at, pair], dst_ref=recv_f.at[at, pair],
            send_sem=sf_sem.at[at, level], recv_sem=rf_sem.at[at, level],
            device_id=(partner(level),), device_id_type=MESH,
        )

    def adjoint_copy(at, level):
        pair = pl.ds(2 * level, 2)
        return pltpu.make_async_remote_copy(
            src_ref=send_b.at[at, pair], dst_ref=recv_b.at[at, pair],
            send_sem=sb_sem.at[at, level], recv_sem=rb_sem.at[at, level],
            device_id=(partner(level),), device_id_type=MESH,
        )

    def send_forward(at):
        for k in range(coups):
            send_f[at, k] = field[at, sends[0, k]]
        for level in range(rounds):
            forward_copy(at, level).start()

    def send_adjoint(at):
        for k in range(coups):
            term = dot(back[at, rows[0, k]], cross[0, k // 2, k % 2])
            send_b[at, k] = (term * pair_ref[0, k // 2].astype(F32)).astype(BF16)
        for level in range(rounds):
            adjoint_copy(at, level).start()

    def take_forward(at):
        for level in range(rounds):
            forward_copy(at, level).wait_recv()
        for k in range(coups):
            term = dot(recv_f[at, k], cross_t[k]) * pair_ref[0, k // 2].astype(F32)
            coup[k] = term + coup[rows[1, k]]

    def take_adjoint(at):
        for level in range(rounds):
            adjoint_copy(at, level).wait_recv()
        for k in range(coups):
            coup[k] = recv_b[at, k].astype(F32) + coup[sends[1, k]]

    def forward_rows(at, low, high, fresh, unroll):
        def body(i, carry):
            values = jnp.concatenate([field[at, col[i, n]] for n in range(nz)], axis=1)
            if fresh:
                tiles = []
                for n in range(nz):
                    tile = lap[i, n].T
                    lap_t[i, n] = tile
                    tiles.append(tile)
            else:
                tiles = [lap_t[i, n] for n in range(nz)]
            summed = dot(values, jnp.concatenate(tiles, axis=0)) + coup[idx[6, i]]
            if at > 0:
                summed = 2.0 * summed - field[at - 1, i].astype(F32)
            field[at + 1, i] = (summed * mask_of(i)).astype(BF16)
            return carry

        lax.fori_loop(low, high, body, 0, unroll=unroll)

    def adjoint_chains(at):
        def body(i, carry):
            tiles = jnp.concatenate([lap[i, n] for n in range(nz)], axis=1)
            terms = dot(back[at, i], tiles)
            for n in range(nz):
                chains[n][i] = terms[:, n * block : (n + 1) * block] + chains[n][idx[n, i]]
            return carry

        lax.fori_loop(0, blocks, body, 0, unroll=16)

    def adjoint_sums(at):
        def body(i, carry):
            summed = coup[idx[7, i]]
            for n in range(nz):
                summed = summed + chains[n][idx[nz + n, i]]
            lifted = dot(cheb_ref[2 - at], up[i])
            if at < 2:
                summed = lifted + 2.0 * summed
            else:
                summed = lifted + summed
            if at > 0:
                summed = summed - back[at - 1, i].astype(F32)
            summed = (summed * mask_of(i)).astype(BF16)
            if at < 2:
                back[at + 1, i] = summed
            else:
                gradx[:, lanes(i)] = summed
            return carry

        lax.fori_loop(0, blocks, body, 0, unroll=8)

    loads[0].wait()

    def zeroth_body(i, carry):
        field[0, i] = feat[:, lanes(i)] * mask_of(i).astype(BF16)
        return carry

    lax.fori_loop(0, blocks, zeroth_body, 0, unroll=8)
    pl.semaphore_wait(barrier, rounds + GROUP - 1 + far_size - 1)
    send_forward(0)

    loads[1].wait()

    def upstream_body(i, carry):
        value = cot[:, lanes(i)] * mask_of(i).astype(BF16)
        up[i] = value
        up_t[i] = value.T
        back[0, i] = (dot(cheb_ref[3], value) * mask_of(i)).astype(BF16)
        return carry

    lax.fori_loop(0, blocks, upstream_body, 0, unroll=8)
    loads[2].wait()
    for k in range(coups):
        cross_t[k] = cross[0, k // 2, k % 2].T
    send_adjoint(0)
    idx_copy.wait()

    take_forward(0)
    for part_at in range(CHUNKS):
        lap_load(part_at).wait()
        forward_rows(0, part_at * per, (part_at + 1) * per, True, per)
    send_forward(1)
    adjoint_chains(0)
    take_adjoint(0)
    adjoint_sums(0)
    send_adjoint(1)
    take_forward(1)
    forward_rows(1, 0, blocks, False, 16)
    send_forward(2)
    adjoint_chains(1)
    take_adjoint(1)
    adjoint_sums(1)
    send_adjoint(2)
    take_forward(2)
    forward_rows(2, 0, blocks, False, 16)

    def weight_body(i, total):
        values = jnp.concatenate(
            [jnp.concatenate([field[k, 2 * i + h] for k in range(4)], axis=0) for h in range(2)], axis=1
        )
        ups = jnp.concatenate([up_t[2 * i + h] for h in range(2)], axis=0)
        return total + dot(values, ups)

    total = lax.fori_loop(0, blocks // 2, weight_body, jnp.zeros((4 * width, width), F32), unroll=4)
    half = 2 * width
    part[...] = jnp.concatenate([total[:half], total[half:]], axis=1)

    def near_copy(step, source, target, ssem, rsem, spread):
        peer_at = (near + step) % GROUP
        src = source.at[pl.ds(pl.multiple_of(peer_at * 8, 8), 8)] if spread else source
        return pltpu.make_async_remote_copy(
            src_ref=src, dst_ref=target.at[near], send_sem=ssem.at[step], recv_sem=rsem.at[near],
            device_id=(near_peer(step),), device_id_type=MESH,
        )

    def far_copy(step):
        return pltpu.make_async_remote_copy(
            src_ref=mine2, dst_ref=got2.at[far], send_sem=s2_sem.at[step], recv_sem=r2_sem.at[far],
            device_id=(far_peer(step),), device_id_type=MESH,
        )

    def arrival(source, target, at, ssem, rsem, peer):
        return pltpu.make_async_remote_copy(
            src_ref=source, dst_ref=target.at[at], send_sem=ssem.at[0], recv_sem=rsem.at[at],
            device_id=(peer,), device_id_type=MESH,
        )

    @pl.loop(1, GROUP)
    def _(step):
        near_copy(step, part, got1, s1_sem, r1_sem, True).start()

    got1[near] = part[pl.ds(pl.multiple_of(near * 8, 8), 8), :]

    def output_body(i, carry):
        values = jnp.concatenate([field[k, i] for k in range(4)], axis=0)
        conv[:, lanes(i)] = (dot(cheb_all, values) * mask_of(i)).astype(BF16)
        return carry

    lax.fori_loop(0, blocks, output_body, 0, unroll=8)
    conv_out = pltpu.make_async_copy(conv, conv_hbm, out_sem.at[0])
    conv_out.start()

    @pl.loop(1, GROUP)
    def _(step):
        arrival(part.at[pl.ds(0, 8)], got1, (near + step) % GROUP, s1_sem, r1_sem, near_peer(step)).wait_recv()

    summed = got1[0]
    for at in range(1, GROUP):
        summed = summed + got1[at]
    mine2[...] = summed
    got2[far] = summed
    if far_size > 1:
        @pl.loop(1, far_size)
        def _(step):
            far_copy(step).start()

    adjoint_chains(2)

    if far_size > 1:
        @pl.loop(1, far_size)
        def _(step):
            arrival(mine2, got2, (far + step) % far_size, s2_sem, r2_sem, far_peer(step)).wait_recv()

    summed = got2[0]
    for at in range(1, far_size):
        summed = summed + got2[at]
    mine3[...] = summed
    got3[near] = summed

    @pl.loop(1, GROUP)
    def _(step):
        near_copy(step, mine3, got3, s3_sem, r3_sem, False).start()

    take_adjoint(2)
    adjoint_sums(2)
    gradx_out = pltpu.make_async_copy(gradx, gradx_hbm, out_sem.at[1])
    gradx_out.start()

    @pl.loop(1, GROUP)
    def _(step):
        arrival(mine3, got3, (near + step) % GROUP, s3_sem, r3_sem, near_peer(step)).wait_recv()

    whole = jnp.concatenate([got3[at] for at in range(GROUP)], axis=0)
    whole = jnp.concatenate([whole[:, :width], whole[:, width:]], axis=0)
    for k in range(4):
        gradw_ref[k] = whole[k * width : (k + 1) * width]

    for at in range(3):
        for level in range(rounds):
            forward_copy(at, level).wait_send()
            adjoint_copy(at, level).wait_send()

    @pl.loop(1, GROUP)
    def _(step):
        near_copy(step, part, got1, s1_sem, r1_sem, True).wait_send()
        near_copy(step, mine3, got3, s3_sem, r3_sem, False).wait_send()

    if far_size > 1:
        @pl.loop(1, far_size)
        def _(step):
            far_copy(step).wait_send()

    conv_out.wait()
    gradx_out.wait()


def local(size, features, cheb_weight, lap_tiles, col_index, cross_tiles, send_index, row_index, pair_on, blk_live, cotangent):
    width, pixels = features.shape
    blocks, nz, block = lap_tiles.shape[:3]
    rounds, hb = cross_tiles.shape[1:3]
    coups = rounds * hb
    hbm = pl.BlockSpec(memory_space=pl.ANY)
    smem = pl.BlockSpec(memory_space=pltpu.SMEM)
    vmem = pl.BlockSpec(memory_space=pltpu.VMEM)
    dma = pltpu.SemaphoreType.DMA
    far_size = size // GROUP
    return pl.pallas_call(
        functools.partial(kernel, size),
        out_shape=(
            jax.ShapeDtypeStruct((width, pixels), BF16),
            jax.ShapeDtypeStruct((width, pixels), BF16),
            jax.ShapeDtypeStruct(cheb_weight.shape, F32),
        ),
        in_specs=[hbm, vmem, hbm, vmem, smem, hbm, smem, smem, smem, smem, hbm],
        out_specs=(hbm, hbm, vmem),
        scratch_shapes=[
            pltpu.VMEM((width, pixels), BF16),
            pltpu.VMEM((width, pixels), BF16),
            pltpu.VMEM((blocks, nz, block, block), BF16),
            pltpu.VMEM((blocks, nz, block, block), BF16),
            pltpu.VMEM((1, rounds, hb, block, block), BF16),
            pltpu.VMEM((coups, block, block), BF16),
            pltpu.VMEM((4, blocks, width, block), BF16),
            pltpu.VMEM((3, blocks, width, block), BF16),
            pltpu.VMEM((blocks, width, block), BF16),
            pltpu.VMEM((blocks, block, width), BF16),
            pltpu.VMEM((blocks + 1, width, block), F32),
            pltpu.VMEM((blocks + 1, width, block), F32),
            pltpu.VMEM((blocks + 1, width, block), F32),
            pltpu.VMEM((coups + 1, width, block), F32),
            pltpu.VMEM((3, coups, width, block), BF16),
            pltpu.VMEM((3, coups, width, block), BF16),
            pltpu.VMEM((3, coups, width, block), BF16),
            pltpu.VMEM((3, coups, width, block), BF16),
            pltpu.VMEM((width, pixels), BF16),
            pltpu.VMEM((width, pixels), BF16),
            pltpu.VMEM((8, 128), I32),
            pltpu.SMEM((8, 128), I32),
            pltpu.SMEM((2, coups), I32),
            pltpu.SMEM((2, coups), I32),
            pltpu.VMEM((2 * width, 2 * width), F32),
            pltpu.VMEM((GROUP, 8, 2 * width), F32),
            pltpu.VMEM((8, 2 * width), F32),
            pltpu.VMEM((far_size, 8, 2 * width), F32),
            pltpu.VMEM((8, 2 * width), F32),
            pltpu.VMEM((GROUP, 8, 2 * width), F32),
            dma((3,)),
            dma((CHUNKS,)),
            dma,
            dma((2,)),
            dma((3, rounds)),
            dma((3, rounds)),
            dma((3, rounds)),
            dma((3, rounds)),
            dma((GROUP,)),
            dma((GROUP,)),
            dma((far_size,)),
            dma((far_size,)),
            dma((GROUP,)),
            dma((GROUP,)),
        ],
        compiler_params=pltpu.CompilerParams(
            collective_id=0, has_side_effects=True, vmem_limit_bytes=56 * 2**20
        ),
    )(features, cheb_weight, lap_tiles, col_index, col_index, cross_tiles, send_index, row_index, pair_on, blk_live, cotangent)


def solution(mesh):
    dom = P("dom")
    return jax.shard_map(
        functools.partial(local, mesh.shape["dom"]),
        mesh=mesh,
        in_specs=(P(None, "dom"), P(), dom, dom, dom, dom, dom, dom, dom, P(None, "dom")),
        out_specs=(P(None, "dom"), P(None, "dom"), P()),
        check_vma=False,
    )
```

profile of v0, /device:TPU:1, one launch (start us, length us, event | category | flops | bytes accessed | tf_op | source)
XLA Modules:
  0.0 85.4 jit_solution(18103742250143048117)
XLA Ops:
  1.3 1.4 %copy.15.send_ref = s32[1,5,2]{2,1,0:T(8,128)} copy(s32[1,5,2]{1,2,0:T(2,128)} %param.15) | data formatting | bytes 80 | tf_op args[5]
  2.6 1.4 %copy.16.row_ref = s32[1,5,2]{2,1,0:T(8,128)} copy(s32[1,5,2]{1,2,0:T(2,128)} %param.16) | data formatting | bytes 80 | tf_op args[6]
  4.0 1.4 %copy.13.col_vmem.col = s32[64,3]{1,0:T(8,128)} copy(s32[64,3]{0,1:T(4,128)} %param.13) | data formatting | bytes 1536 | tf_op args[3]
  5.4 73.9 %shard_map.121 = (bf16[64,8192]{1,0:T(8,128)(2,1)}, bf16[64,8192]{1,0:T(8,128)(2,1)}, f32[4,64,64]{2,1,0:T(8,128)}) custom-call(bf16[64,8192]{1,0:T(8,128)(2,1)} %feat_hbm.1, bf16[4,64,64]{2,1,0:T(8,128)(2,1)} %cheb_ref.1, bf16[64,3,128,128]{3,2,1,0:T(8,128)(2,1)} %lap_hbm.1, s32[64,3]{1,0:T(8,128)} %copy.13.col_vmem.col, s32[64,3]{1,0:T(8,128)} %copy.13.col_vmem.col, ...), custom_call_target="tpu_custom_call" | custom-call | tf_op jit(solution)/shard_map/pallas_call | solution.py:390
  79.3 2.3 %copy.21 = bf16[64,8192]{1,0:T(8,128)(2,1)} copy(bf16[64,8192]{1,0:T(8,128)(2,1)} %get-tuple-element.6) | data formatting | bytes 2097152
  81.6 2.3 %copy.22 = bf16[64,8192]{1,0:T(8,128)(2,1)} copy(bf16[64,8192]{1,0:T(8,128)(2,1)} %get-tuple-element.7) | data formatting | bytes 2097152
  83.8 1.6 %copy.23 = f32[4,64,64]{2,1,0:T(8,128)} copy(f32[4,64,64]{2,1,0:T(8,128)} %get-tuple-element.8) | data formatting | bytes 131072
where the time goes:
time: 85.7 us; the launch traced here: 85.4 us
  Pallas kernels  73.9 us (86%)
  local copies, waits for them, and re-layouts  10.2 us (12%)
  between operations  1.29 us (2%)
    pallas_call x1, Pallas kernels, local(): pl.pallas_call(functools.partial(kernel, size), out_shape=(jax.ShapeDtype...  73.9 us
    unnamed x6, local copies, waits for them, and re-layouts  10.2 us

commit v1 on v0

--- a/solution.py
+++ b/solution.py
@@ -12,7 +12,12 @@
 I32 = jnp.int32
 MESH = pl.DeviceIdType.MESH
 GROUP = 16
-CHUNKS = 8
+CHUNKS = 4
+FIRST = 16
+WIDE = 64
+SUMS = 64
+DENSE = 64
+WEIGHT = 32
 
 
 def dot(a, b):
@@ -34,7 +39,7 @@
     size,
     feat_hbm, cheb_ref, lap_hbm, col_vmem, col, cross_hbm, send_ref, row_ref, pair_ref, live_ref, cot_hbm,
     conv_hbm, gradx_hbm, gradw_ref,
-    feat, cot, lap, lap_t, cross, cross_t, field, back, up, up_t, chain0, chain1, chain2, coup,
+    feat, cot, lap, lap_t, cross, cross_t, field0, field1, field2, field3, back0, back1, back2, both_t, chain0, chain1, chain2, coup_f, coup_b,
     send_f, recv_f, send_b, recv_b, conv, gradx, idx_v, idx, sends, rows, part, got1, mine2, got2, mine3, got3,
     load_sem, lap_sem, idx_sem, out_sem, sf_sem, rf_sem, sb_sem, rb_sem,
     s1_sem, r1_sem, s2_sem, r2_sem, s3_sem, r3_sem,
@@ -44,6 +49,8 @@
     rounds = 5
     coups = 2 * rounds
     chains = (chain0, chain1, chain2)
+    field = (field0, field1, field2, field3)
+    back = (back0, back1, back2)
     me = lax.axis_index("dom")
     near, far = me % GROUP, me // GROUP
     far_size = size // GROUP
@@ -93,25 +100,25 @@
         return (i < live).astype(F32)
 
     for k in range(coups):
-        sends[0, k] = small_mod(send_ref[0, k // 2, k % 2], live, blocks - 1)
-        rows[0, k] = small_mod(row_ref[0, k // 2, k % 2], live, blocks - 1)
+        sends[0, k] = small_mod(send_ref[0, k % 2, k // 2], live, blocks - 1)
+        rows[0, k] = small_mod(row_ref[0, k % 2, k // 2], live, blocks - 1)
     for table in (sends, rows):
         for k in range(coups):
             before = jnp.int32(coups)
             for other in range(k):
                 before = jnp.where(table[0, other] == table[0, k], other, before)
             table[1, k] = before
-    at_sub = lax.broadcasted_iota(I32, (blocks, 128), 0)
-    at_lane = lax.broadcasted_iota(I32, (blocks, 128), 1)
+    at_sub = lax.broadcasted_iota(I32, (blocks, blocks), 0)
+    at_lane = lax.broadcasted_iota(I32, (blocks, blocks), 1)
     lane = lax.broadcasted_iota(I32, (1, 128), 1)
     for n in range(nz):
-        cols = jnp.broadcast_to(col_vmem[:, n : n + 1], (blocks, 128))
-        turned = jnp.sum(jnp.where(at_sub == at_lane, cols, 0), axis=0, keepdims=True)
+        turned = jnp.broadcast_to(col_vmem[n : n + 1, :], (blocks, blocks))
+        cols = jnp.sum(jnp.where(at_sub == at_lane, turned, 0), axis=1, keepdims=True)
         same = (cols == turned) & (at_sub < at_lane)
         prev = jnp.max(jnp.where(same, at_sub, -1), axis=0, keepdims=True)
         last = jnp.max(jnp.where(cols == at_lane, at_sub, -1), axis=0, keepdims=True)
-        idx_v[n : n + 1, :] = jnp.where(prev < 0, blocks, prev)
-        idx_v[nz + n : nz + n + 1, :] = jnp.where(last < 0, blocks, last)
+        idx_v[n : n + 1, :blocks] = jnp.where(prev < 0, blocks, prev)
+        idx_v[nz + n : nz + n + 1, :blocks] = jnp.where(last < 0, blocks, last)
     for at, table in ((6, rows), (7, sends)):
         last = jnp.full((1, 128), coups, I32)
         for k in range(coups):
@@ -123,9 +130,11 @@
     zero_block = jnp.zeros((width, block), F32)
     for chain in chains:
         chain[blocks] = zero_block
-    coup[coups] = zero_block
+    coup_f[coups] = zero_block
+    coup_b[coups] = zero_block
     cheb = cheb_ref[...]
     cheb_all = jnp.concatenate([cheb[k].T for k in range(4)], axis=1)
+    cheb_back = jnp.concatenate([cheb[k] for k in range(4)], axis=1)
 
     def lanes(i):
         return pl.ds(pl.multiple_of(i * block, block), block)
@@ -146,15 +155,13 @@
             device_id=(partner(level),), device_id_type=MESH,
         )
 
-    def send_forward(at):
-        for k in range(coups):
-            send_f[at, k] = field[at, sends[0, k]]
+    def start_forward(at):
         for level in range(rounds):
             forward_copy(at, level).start()
 
-    def send_adjoint(at):
+    def send_adjoint(at, block_of):
         for k in range(coups):
-            term = dot(back[at, rows[0, k]], cross[0, k // 2, k % 2])
+            term = dot(block_of(rows[0, k]), cross[0, k // 2, k % 2])
             send_b[at, k] = (term * pair_ref[0, k // 2].astype(F32)).astype(BF16)
         for level in range(rounds):
             adjoint_copy(at, level).start()
@@ -164,119 +171,124 @@
             forward_copy(at, level).wait_recv()
         for k in range(coups):
             term = dot(recv_f[at, k], cross_t[k]) * pair_ref[0, k // 2].astype(F32)
-            coup[k] = term + coup[rows[1, k]]
+            coup_f[k] = term + coup_f[rows[1, k]]
 
     def take_adjoint(at):
         for level in range(rounds):
             adjoint_copy(at, level).wait_recv()
         for k in range(coups):
-            coup[k] = recv_b[at, k].astype(F32) + coup[sends[1, k]]
-
-    def forward_rows(at, low, high, fresh, unroll):
-        def body(i, carry):
-            values = jnp.concatenate([field[at, col[i, n]] for n in range(nz)], axis=1)
-            if fresh:
-                tiles = []
-                for n in range(nz):
-                    tile = lap[i, n].T
-                    lap_t[i, n] = tile
-                    tiles.append(tile)
-            else:
-                tiles = [lap_t[i, n] for n in range(nz)]
-            summed = dot(values, jnp.concatenate(tiles, axis=0)) + coup[idx[6, i]]
-            if at > 0:
-                summed = 2.0 * summed - field[at - 1, i].astype(F32)
-            field[at + 1, i] = (summed * mask_of(i)).astype(BF16)
+            coup_b[k] = recv_b[at, k].astype(F32) + coup_b[sends[1, k]]
+
+    def forward_value(at, i):
+        values = jnp.concatenate([field[at][col[n, i]] for n in range(nz)], axis=1)
+        tiles = jnp.concatenate([lap_t[i, n] for n in range(nz)], axis=0)
+        summed = dot(values, tiles) + coup_f[idx[6, i]]
+        if at > 0:
+            summed = 2.0 * summed - field[at - 1][i].astype(F32)
+        return (summed * mask_of(i)).astype(BF16)
+
+    def adjoint_value(at, i):
+        summed = coup_b[idx[7, i]]
+        for n in range(nz):
+            summed = summed + chains[n][idx[nz + n, i]]
+        if at > 0:
+            summed = 2.0 * summed - back[at - 1][i].astype(F32)
+        return (summed * mask_of(i)).astype(BF16)
+
+    def adjoint_row(at, i, tiles):
+        terms = dot(back[at][i], jnp.concatenate(tiles, axis=1))
+        for n in range(nz):
+            chains[n][i] = terms[:, n * block : (n + 1) * block] + chains[n][idx[n, i]]
+
+    def first_chains(low):
+        def body(step, carry):
+            i = low + step
+            tiles = [lap[i, n] for n in range(nz)]
+            for n in range(nz):
+                lap_t[i, n] = tiles[n].T
+            adjoint_row(0, i, tiles)
             return carry
 
-        lax.fori_loop(low, high, body, 0, unroll=unroll)
+        lax.fori_loop(0, per, body, 0, unroll=FIRST)
 
     def adjoint_chains(at):
         def body(i, carry):
-            tiles = jnp.concatenate([lap[i, n] for n in range(nz)], axis=1)
-            terms = dot(back[at, i], tiles)
-            for n in range(nz):
-                chains[n][i] = terms[:, n * block : (n + 1) * block] + chains[n][idx[n, i]]
+            adjoint_row(at, i, [lap[i, n] for n in range(nz)])
             return carry
 
-        lax.fori_loop(0, blocks, body, 0, unroll=16)
-
-    def adjoint_sums(at):
+        lax.fori_loop(0, blocks, body, 0, unroll=WIDE)
+
+    def forward_rows(at):
         def body(i, carry):
-            summed = coup[idx[7, i]]
-            for n in range(nz):
-                summed = summed + chains[n][idx[nz + n, i]]
-            lifted = dot(cheb_ref[2 - at], up[i])
-            if at < 2:
-                summed = lifted + 2.0 * summed
-            else:
-                summed = lifted + summed
-            if at > 0:
-                summed = summed - back[at - 1, i].astype(F32)
-            summed = (summed * mask_of(i)).astype(BF16)
-            if at < 2:
-                back[at + 1, i] = summed
-            else:
-                gradx[:, lanes(i)] = summed
+            field[at + 1][i] = forward_value(at, i)
             return carry
 
-        lax.fori_loop(0, blocks, body, 0, unroll=8)
+        lax.fori_loop(0, blocks, body, 0, unroll=WIDE)
+
+    def send_forward(at):
+        for k in range(coups):
+            send_f[at, k] = forward_value(at - 1, sends[0, k])
+        start_forward(at)
 
     loads[0].wait()
 
     def zeroth_body(i, carry):
-        field[0, i] = feat[:, lanes(i)] * mask_of(i).astype(BF16)
+        field[0][i] = feat[:, lanes(i)] * mask_of(i).astype(BF16)
         return carry
 
-    lax.fori_loop(0, blocks, zeroth_body, 0, unroll=8)
+    lax.fori_loop(0, blocks, zeroth_body, 0, unroll=16)
+    for k in range(coups):
+        send_f[0, k] = field[0][sends[0, k]]
     pl.semaphore_wait(barrier, rounds + GROUP - 1 + far_size - 1)
-    send_forward(0)
-
+    start_forward(0)
     loads[1].wait()
 
     def upstream_body(i, carry):
-        value = cot[:, lanes(i)] * mask_of(i).astype(BF16)
-        up[i] = value
-        up_t[i] = value.T
-        back[0, i] = (dot(cheb_ref[3], value) * mask_of(i)).astype(BF16)
+        back[0][i] = cot[:, lanes(i)] * mask_of(i).astype(BF16)
         return carry
 
-    lax.fori_loop(0, blocks, upstream_body, 0, unroll=8)
+    lax.fori_loop(0, blocks, upstream_body, 0, unroll=16)
     loads[2].wait()
+    send_adjoint(0, lambda i: back[0][i])
     for k in range(coups):
         cross_t[k] = cross[0, k // 2, k % 2].T
-    send_adjoint(0)
     idx_copy.wait()
 
+    @pl.loop(0, CHUNKS)
+    def _(part_at):
+        lap_load(part_at).wait()
+        first_chains(part_at * per)
+
     take_forward(0)
-    for part_at in range(CHUNKS):
-        lap_load(part_at).wait()
-        forward_rows(0, part_at * per, (part_at + 1) * per, True, per)
     send_forward(1)
-    adjoint_chains(0)
+
+    forward_rows(0)
     take_adjoint(0)
-    adjoint_sums(0)
-    send_adjoint(1)
+    send_adjoint(1, lambda i: adjoint_value(0, i))
+
+    def adjoint_first_body(i, total):
+        value = adjoint_value(0, i)
+        back[1][i] = value
+        turned = jnp.concatenate([back[0][i], value], axis=0).T
+        both_t[i] = turned
+        return total + dot(jnp.concatenate([field[0][i], field[1][i]], axis=0), turned)
+
+    low = lax.fori_loop(0, blocks, adjoint_first_body, jnp.zeros((2 * width, 2 * width), F32), unroll=SUMS)
+    adjoint_chains(1)
     take_forward(1)
-    forward_rows(1, 0, blocks, False, 16)
     send_forward(2)
-    adjoint_chains(1)
-    take_adjoint(1)
-    adjoint_sums(1)
-    send_adjoint(2)
-    take_forward(2)
-    forward_rows(2, 0, blocks, False, 16)
-
-    def weight_body(i, total):
-        values = jnp.concatenate(
-            [jnp.concatenate([field[k, 2 * i + h] for k in range(4)], axis=0) for h in range(2)], axis=1
-        )
-        ups = jnp.concatenate([up_t[2 * i + h] for h in range(2)], axis=0)
-        return total + dot(values, ups)
-
-    total = lax.fori_loop(0, blocks // 2, weight_body, jnp.zeros((4 * width, width), F32), unroll=4)
-    half = 2 * width
-    part[...] = jnp.concatenate([total[:half], total[half:]], axis=1)
+
+    forward_rows(1)
+
+    def second_terms(i, total):
+        values = jnp.concatenate([field[2][2 * i + h] for h in range(2)], axis=1)
+        return total + dot(values, jnp.concatenate([both_t[2 * i + h] for h in range(2)], axis=0))
+
+    zero = jnp.zeros((width, 2 * width), F32)
+    high = lax.fori_loop(0, blocks // 2, second_terms, zero, unroll=WEIGHT)
+
+    last_term = 2.0 * high[:, width:] - low[width:, :width]
+    part[...] = jnp.concatenate([low[:, :width], jnp.concatenate([high[:, :width], last_term], axis=0)], axis=1)
 
     def near_copy(step, source, target, ssem, rsem, spread):
         peer_at = (near + step) % GROUP
@@ -303,15 +315,18 @@
         near_copy(step, part, got1, s1_sem, r1_sem, True).start()
 
     got1[near] = part[pl.ds(pl.multiple_of(near * 8, 8), 8), :]
-
-    def output_body(i, carry):
-        values = jnp.concatenate([field[k, i] for k in range(4)], axis=0)
-        conv[:, lanes(i)] = (dot(cheb_all, values) * mask_of(i)).astype(BF16)
+    take_adjoint(1)
+    send_adjoint(2, lambda i: adjoint_value(1, i))
+
+    def adjoint_second_body(i, carry):
+        back[2][i] = adjoint_value(1, i)
         return carry
 
-    lax.fori_loop(0, blocks, output_body, 0, unroll=8)
-    conv_out = pltpu.make_async_copy(conv, conv_hbm, out_sem.at[0])
-    conv_out.start()
+    lax.fori_loop(0, blocks, adjoint_second_body, 0, unroll=SUMS)
+    adjoint_chains(2)
+    take_forward(2)
+
+    forward_rows(2)
 
     @pl.loop(1, GROUP)
     def _(step):
@@ -327,7 +342,26 @@
         def _(step):
             far_copy(step).start()
 
-    adjoint_chains(2)
+
+    def output_body(i, carry):
+        values = jnp.concatenate([field[k][i] for k in range(4)], axis=0)
+        conv[:, lanes(i)] = (dot(cheb_all, values) * mask_of(i)).astype(BF16)
+        return carry
+
+    lax.fori_loop(0, blocks, output_body, 0, unroll=DENSE)
+    conv_out = pltpu.make_async_copy(conv, conv_hbm, out_sem.at[0])
+    conv_out.start()
+    take_adjoint(2)
+
+    def gradient_body(i, carry):
+        third = adjoint_value(2, i)
+        values = jnp.concatenate([back[0][i], back[1][i], back[2][i], third], axis=0)
+        gradx[:, lanes(i)] = (dot(cheb_back, values) * mask_of(i)).astype(BF16)
+        return carry
+
+    lax.fori_loop(0, blocks, gradient_body, 0, unroll=DENSE)
+    gradx_out = pltpu.make_async_copy(gradx, gradx_hbm, out_sem.at[1])
+    gradx_out.start()
 
     if far_size > 1:
         @pl.loop(1, far_size)
@@ -344,11 +378,6 @@
     def _(step):
         near_copy(step, mine3, got3, s3_sem, r3_sem, False).start()
 
-    take_adjoint(2)
-    adjoint_sums(2)
-    gradx_out = pltpu.make_async_copy(gradx, gradx_hbm, out_sem.at[1])
-    gradx_out.start()
-
     @pl.loop(1, GROUP)
     def _(step):
         arrival(mine3, got3, (near + step) % GROUP, s3_sem, r3_sem, near_peer(step)).wait_recv()
@@ -375,6 +404,32 @@
 
     conv_out.wait()
     gradx_out.wait()
+
+
+PIECES = 4
+
+
+def handed_on(conv_in, gradx_in, gradw_in, conv_out, gradx_out, gradw_out, conv, gradx, gradw, in_sem, out_sem):
+    moves = []
+    for at, (source, held, target) in enumerate(
+        ((gradw_in, gradw, gradw_out), (conv_in, conv, conv_out), (gradx_in, gradx, gradx_out))
+    ):
+        each = source.shape[0] // PIECES
+        for piece in range(PIECES):
+            where = pl.ds(piece * each, each)
+            moves.append(
+                (
+                    pltpu.make_async_copy(source.at[where], held.at[where], in_sem.at[at, piece]),
+                    pltpu.make_async_copy(held.at[where], target.at[where], out_sem.at[at, piece]),
+                )
+            )
+    for first, _ in moves:
+        first.start()
+    for first, second in moves:
+        first.wait()
+        second.start()
+    for _, second in moves:
+        second.wait()
 
 
 def local(size, features, cheb_weight, lap_tiles, col_index, cross_tiles, send_index, row_index, pair_on, blk_live, cotangent):
@@ -387,7 +442,7 @@
     vmem = pl.BlockSpec(memory_space=pltpu.VMEM)
     dma = pltpu.SemaphoreType.DMA
     far_size = size // GROUP
-    return pl.pallas_call(
+    results = pl.pallas_call(
         functools.partial(kernel, size),
         out_shape=(
             jax.ShapeDtypeStruct((width, pixels), BF16),
@@ -403,13 +458,12 @@
             pltpu.VMEM((blocks, nz, block, block), BF16),
             pltpu.VMEM((1, rounds, hb, block, block), BF16),
             pltpu.VMEM((coups, block, block), BF16),
-            pltpu.VMEM((4, blocks, width, block), BF16),
-            pltpu.VMEM((3, blocks, width, block), BF16),
-            pltpu.VMEM((blocks, width, block), BF16),
-            pltpu.VMEM((blocks, block, width), BF16),
+            *[pltpu.VMEM((blocks, width, block), BF16)] * 7,
+            pltpu.VMEM((blocks, block, 2 * width), BF16),
             pltpu.VMEM((blocks + 1, width, block), F32),
             pltpu.VMEM((blocks + 1, width, block), F32),
             pltpu.VMEM((blocks + 1, width, block), F32),
+            pltpu.VMEM((coups + 1, width, block), F32),
             pltpu.VMEM((coups + 1, width, block), F32),
             pltpu.VMEM((3, coups, width, block), BF16),
             pltpu.VMEM((3, coups, width, block), BF16),
@@ -445,7 +499,14 @@
         compiler_params=pltpu.CompilerParams(
             collective_id=0, has_side_effects=True, vmem_limit_bytes=56 * 2**20
         ),
-    )(features, cheb_weight, lap_tiles, col_index, col_index, cross_tiles, send_index, row_index, pair_on, blk_live, cotangent)
+    )(features, cheb_weight, lap_tiles, col_index.T, col_index.T, cross_tiles, send_index.swapaxes(1, 2), row_index.swapaxes(1, 2), pair_on, blk_live, cotangent)
+    return pl.pallas_call(
+        handed_on,
+        out_shape=tuple(jax.ShapeDtypeStruct(each.shape, each.dtype) for each in results),
+        in_specs=[hbm] * 3,
+        out_specs=(hbm,) * 3,
+        scratch_shapes=[pltpu.VMEM(each.shape, each.dtype) for each in results] + [dma((3, PIECES)), dma((3, PIECES))],
+    )(*results)
 
 
 def solution(mesh):

time: 85.7 us -> 44.7 us (0.52)
  Pallas kernels: 73.9 us -> 43.2 us
  local copies, waits for them, and re-layouts: 10.2 us -> 0 us
    pallas_call x1, Pallas kernels: 73.9 us -> 40.7 us  [local(): pl.pallas_call(functools.partial(kernel, size), out_shape=(jax.ShapeDtype...]
    unnamed x6 -> x0, local copies, waits for them, and re-layouts: 10.2 us -> none
    pallas_call x0 -> x1, Pallas kernels: none -> 2.55 us  [local(): pl.pallas_call(handed_on, out_shape=tuple((jax.ShapeDtypeStruct(each.shap...]
where the time goes in v1:
time: 44.7 us; the launch traced here: 44.5 us
  Pallas kernels  43.2 us (97%)
  between operations  1.29 us (3%)
    pallas_call x1, Pallas kernels, local(): pl.pallas_call(functools.partial(kernel, size), out_shape=(jax.ShapeDtype...  40.7 us
    pallas_call x1, Pallas kernels, local(): pl.pallas_call(handed_on, out_shape=tuple((jax.ShapeDtypeStruct(each.shap...  2.55 us

profile of v1, /device:TPU:1, one launch (start us, length us, event | category | flops | bytes accessed | tf_op | source)
XLA Modules:
  0.0 44.5 jit_solution(18425775290435540875)
XLA Ops:
  1.3 40.7 %shard_map.121 = (bf16[64,8192]{1,0:T(8,128)(2,1)}, bf16[64,8192]{1,0:T(8,128)(2,1)}, f32[4,64,64]{2,1,0:T(8,128)}) custom-call(bf16[64,8192]{1,0:T(8,128)(2,1)} %feat_hbm.1, bf16[4,64,64]{2,1,0:T(8,128)(2,1)} %cheb_ref.1, bf16[64,3,128,128]{3,2,1,0:T(8,128)(2,1)} %lap_hbm.1, s32[3,64]{1,0:T(4,128)} %bitcast.3, s32[3,64]{1,0:T(4,128)} %bitcast.4, ...), custom_call_target="tpu_custom_call" | custom-call | tf_op jit(solution)/shard_map/pallas_call | solution.py:445
  42.0 2.5 %shard_map.122 = (bf16[64,8192]{1,0:T(8,128)(2,1)}, bf16[64,8192]{1,0:T(8,128)(2,1)}, f32[4,64,64]{2,1,0:T(8,128)}) custom-call(bf16[64,8192]{1,0:T(8,128)(2,1)} %get-tuple-element.6.conv_in, bf16[64,8192]{1,0:T(8,128)(2,1)} %get-tuple-element.7.gradx_in, f32[4,64,64]{2,1,0:T(8,128)} %get-tuple-element.8.gradw_in), custom_call_target="tpu_custom_call" | custom-call | tf_op jit(solution)/shard_map/pallas_call | solution.py:503

commit v2 on v1

--- a/solution.py
+++ b/solution.py
@@ -85,12 +85,12 @@
     for level in range(rounds):
         pl.semaphore_signal(barrier, inc=1, device_id=(partner(level),), device_id_type=MESH)
 
-    @pl.loop(1, GROUP)
+    @pl.loop(1, GROUP, unroll=True)
     def _(step):
         pl.semaphore_signal(barrier, inc=1, device_id=(near_peer(step),), device_id_type=MESH)
 
     if far_size > 1:
-        @pl.loop(1, far_size)
+        @pl.loop(1, far_size, unroll=True)
         def _(step):
             pl.semaphore_signal(barrier, inc=1, device_id=(far_peer(step),), device_id_type=MESH)
 
@@ -143,7 +143,7 @@
         pair = pl.ds(2 * level, 2)
         return pltpu.make_async_remote_copy(
             src_ref=send_f.at[at, pair], dst_ref=recv_f.at[at, pair],
-            send_sem=sf_sem.at[at, level], recv_sem=rf_sem.at[at, level],
+            send_sem=sf_sem.at[at], recv_sem=rf_sem.at[at],
             device_id=(partner(level),), device_id_type=MESH,
         )
 
@@ -151,31 +151,41 @@
         pair = pl.ds(2 * level, 2)
         return pltpu.make_async_remote_copy(
             src_ref=send_b.at[at, pair], dst_ref=recv_b.at[at, pair],
-            send_sem=sb_sem.at[at, level], recv_sem=rb_sem.at[at, level],
+            send_sem=sb_sem.at[at], recv_sem=rb_sem.at[at],
             device_id=(partner(level),), device_id_type=MESH,
         )
 
+    def all_of(source, target, ssem, rsem):
+        return pltpu.make_async_remote_copy(
+            src_ref=source, dst_ref=target, send_sem=ssem, recv_sem=rsem,
+            device_id=(partner(0),), device_id_type=MESH,
+        )
+
+    def all_forward(at):
+        return all_of(send_f.at[at], recv_f.at[at], sf_sem.at[at], rf_sem.at[at])
+
+    def all_adjoint(at):
+        return all_of(send_b.at[at], recv_b.at[at], sb_sem.at[at], rb_sem.at[at])
+
     def start_forward(at):
-        for level in range(rounds):
+        for level in (4, 2, 3, 1, 0):
             forward_copy(at, level).start()
 
     def send_adjoint(at, block_of):
         for k in range(coups):
             term = dot(block_of(rows[0, k]), cross[0, k // 2, k % 2])
             send_b[at, k] = (term * pair_ref[0, k // 2].astype(F32)).astype(BF16)
-        for level in range(rounds):
+        for level in (4, 2, 3, 1, 0):
             adjoint_copy(at, level).start()
 
     def take_forward(at):
-        for level in range(rounds):
-            forward_copy(at, level).wait_recv()
+        all_forward(at).wait_recv()
         for k in range(coups):
             term = dot(recv_f[at, k], cross_t[k]) * pair_ref[0, k // 2].astype(F32)
             coup_f[k] = term + coup_f[rows[1, k]]
 
     def take_adjoint(at):
-        for level in range(rounds):
-            adjoint_copy(at, level).wait_recv()
+        all_adjoint(at).wait_recv()
         for k in range(coups):
             coup_b[k] = recv_b[at, k].astype(F32) + coup_b[sends[1, k]]
 
@@ -294,25 +304,23 @@
         peer_at = (near + step) % GROUP
         src = source.at[pl.ds(pl.multiple_of(peer_at * 8, 8), 8)] if spread else source
         return pltpu.make_async_remote_copy(
-            src_ref=src, dst_ref=target.at[near], send_sem=ssem.at[step], recv_sem=rsem.at[near],
+            src_ref=src, dst_ref=target.at[near], send_sem=ssem, recv_sem=rsem,
             device_id=(near_peer(step),), device_id_type=MESH,
         )
 
     def far_copy(step):
         return pltpu.make_async_remote_copy(
-            src_ref=mine2, dst_ref=got2.at[far], send_sem=s2_sem.at[step], recv_sem=r2_sem.at[far],
+            src_ref=mine2, dst_ref=got2.at[far], send_sem=s2_sem, recv_sem=r2_sem,
             device_id=(far_peer(step),), device_id_type=MESH,
         )
 
-    def arrival(source, target, at, ssem, rsem, peer):
-        return pltpu.make_async_remote_copy(
-            src_ref=source, dst_ref=target.at[at], send_sem=ssem.at[0], recv_sem=rsem.at[at],
-            device_id=(peer,), device_id_type=MESH,
-        )
-
-    @pl.loop(1, GROUP)
-    def _(step):
-        near_copy(step, part, got1, s1_sem, r1_sem, True).start()
+    def slots(target, ssem, rsem):
+        most = target.at[pl.ds(0, target.shape[0] - 1)]
+        return all_of(most, most, ssem, rsem)
+
+    @pl.loop(0, GROUP - 1, unroll=True)
+    def _(at):
+        near_copy(1 + (at + GROUP // 2 - 1) % (GROUP - 1), part, got1, s1_sem, r1_sem, True).start()
 
     got1[near] = part[pl.ds(pl.multiple_of(near * 8, 8), 8), :]
     take_adjoint(1)
@@ -328,19 +336,16 @@
 
     forward_rows(2)
 
-    @pl.loop(1, GROUP)
-    def _(step):
-        arrival(part.at[pl.ds(0, 8)], got1, (near + step) % GROUP, s1_sem, r1_sem, near_peer(step)).wait_recv()
-
+    slots(got1, s1_sem, r1_sem).wait_recv()
     summed = got1[0]
     for at in range(1, GROUP):
         summed = summed + got1[at]
     mine2[...] = summed
     got2[far] = summed
     if far_size > 1:
-        @pl.loop(1, far_size)
-        def _(step):
-            far_copy(step).start()
+        @pl.loop(0, far_size - 1, unroll=True)
+        def _(at):
+            far_copy(1 + (at + far_size // 2 - 1) % (far_size - 1)).start()
 
 
     def output_body(i, carry):
@@ -364,9 +369,7 @@
     gradx_out.start()
 
     if far_size > 1:
-        @pl.loop(1, far_size)
-        def _(step):
-            arrival(mine2, got2, (far + step) % far_size, s2_sem, r2_sem, far_peer(step)).wait_recv()
+        slots(got2, s2_sem, r2_sem).wait_recv()
 
     summed = got2[0]
     for at in range(1, far_size):
@@ -374,33 +377,24 @@
     mine3[...] = summed
     got3[near] = summed
 
-    @pl.loop(1, GROUP)
-    def _(step):
-        near_copy(step, mine3, got3, s3_sem, r3_sem, False).start()
-
-    @pl.loop(1, GROUP)
-    def _(step):
-        arrival(mine3, got3, (near + step) % GROUP, s3_sem, r3_sem, near_peer(step)).wait_recv()
-
+    @pl.loop(0, GROUP - 1, unroll=True)
+    def _(at):
+        near_copy(1 + (at + GROUP // 2 - 1) % (GROUP - 1), mine3, got3, s3_sem, r3_sem, False).start()
+
+    slots(got3, s3_sem, r3_sem).wait_recv()
     whole = jnp.concatenate([got3[at] for at in range(GROUP)], axis=0)
     whole = jnp.concatenate([whole[:, :width], whole[:, width:]], axis=0)
     for k in range(4):
         gradw_ref[k] = whole[k * width : (k + 1) * width]
 
     for at in range(3):
-        for level in range(rounds):
-            forward_copy(at, level).wait_send()
-            adjoint_copy(at, level).wait_send()
-
-    @pl.loop(1, GROUP)
-    def _(step):
-        near_copy(step, part, got1, s1_sem, r1_sem, True).wait_send()
-        near_copy(step, mine3, got3, s3_sem, r3_sem, False).wait_send()
-
+        all_forward(at).wait_send()
+        all_adjoint(at).wait_send()
+
+    slots(got1, s1_sem, r1_sem).wait_send()
+    slots(got3, s3_sem, r3_sem).wait_send()
     if far_size > 1:
-        @pl.loop(1, far_size)
-        def _(step):
-            far_copy(step).wait_send()
+        slots(got2, s2_sem, r2_sem).wait_send()
 
     conv_out.wait()
     gradx_out.wait()
@@ -485,16 +479,16 @@
             dma((CHUNKS,)),
             dma,
             dma((2,)),
-            dma((3, rounds)),
-            dma((3, rounds)),
-            dma((3, rounds)),
-            dma((3, rounds)),
-            dma((GROUP,)),
-            dma((GROUP,)),
-            dma((far_size,)),
-            dma((far_size,)),
-            dma((GROUP,)),
-            dma((GROUP,)),
+            dma((3,)),
+            dma((3,)),
+            dma((3,)),
+            dma((3,)),
+            dma,
+            dma,
+            dma,
+            dma,
+            dma,
+            dma,
         ],
         compiler_params=pltpu.CompilerParams(
             collective_id=0, has_side_effects=True, vmem_limit_bytes=56 * 2**20

time: 44.7 us -> 41.8 us (0.935)
  Pallas kernels: 43.2 us -> 40.4 us
    pallas_call x1, Pallas kernels: 40.7 us -> 37.8 us  [local(): pl.pallas_call(functools.partial(kernel, size), out_shape=(jax.ShapeDtype...]
where the time goes in v2:
time: 41.8 us; the launch traced here: 41.7 us
  Pallas kernels  40.4 us (97%)
  between operations  1.29 us (3%)
    pallas_call x1, Pallas kernels, local(): pl.pallas_call(functools.partial(kernel, size), out_shape=(jax.ShapeDtype...  37.8 us
    pallas_call x1, Pallas kernels, local(): pl.pallas_call(handed_on, out_shape=tuple((jax.ShapeDtypeStruct(each.shap...  2.55 us

profile of v2, /device:TPU:1, one launch (start us, length us, event | category | flops | bytes accessed | tf_op | source)
XLA Modules:
  0.0 41.7 jit_solution(18070808217533695150)
XLA Ops:
  1.3 37.8 %shard_map.121 = (bf16[64,8192]{1,0:T(8,128)(2,1)}, bf16[64,8192]{1,0:T(8,128)(2,1)}, f32[4,64,64]{2,1,0:T(8,128)}) custom-call(bf16[64,8192]{1,0:T(8,128)(2,1)} %feat_hbm.1, bf16[4,64,64]{2,1,0:T(8,128)(2,1)} %cheb_ref.1, bf16[64,3,128,128]{3,2,1,0:T(8,128)(2,1)} %lap_hbm.1, s32[3,64]{1,0:T(4,128)} %bitcast.3, s32[3,64]{1,0:T(4,128)} %bitcast.4, ...), custom_call_target="tpu_custom_call" | custom-call | tf_op jit(solution)/shard_map/pallas_call | solution.py:439
  39.1 2.5 %shard_map.122 = (bf16[64,8192]{1,0:T(8,128)(2,1)}, bf16[64,8192]{1,0:T(8,128)(2,1)}, f32[4,64,64]{2,1,0:T(8,128)}) custom-call(bf16[64,8192]{1,0:T(8,128)(2,1)} %get-tuple-element.6.conv_in, bf16[64,8192]{1,0:T(8,128)(2,1)} %get-tuple-element.7.gradx_in, f32[4,64,64]{2,1,0:T(8,128)} %get-tuple-element.8.gradw_in), custom_call_target="tpu_custom_call" | custom-call | tf_op jit(solution)/shard_map/pallas_call | solution.py:497
